TPU v7x, 32 devices: a whole 2x2x4 slice. The times are simulated.
32 devices in a mesh: groups: 2 (over x), slab: 16 (over z, y, core).
Axes of the slice: x: 2, y: 2, z: 4, core: 2. Of those that a mesh axis runs over, the one named last changes fastest.
Arguments:
- mode_shapes: float32 [16384, 192], P(('groups', 'slab')), parts along dimension 0, may hold values from -6 to 6
- wall_coupling: float32 [16384, 15], P(('groups', 'slab')), parts along dimension 0, may hold values from -3.5 to 3.5
- owner_dev: int32 [16384, 1], P(('groups', 'slab')), parts along dimension 0, may hold values from 0 to 15; in each aligned block of 512 rows (0 to 511, 512 to 1023, ...) at most 64 rows name the same one
- owner_cell: int32 [16384], P(('groups', 'slab')), parts along dimension 0, may hold values from 0 to 2047
- neighbours: int32 [6, 65536], P(None, ('groups', 'slab')), parts along dimension 1, may hold values from -1 to 32767, as said below
- coupling_blocks: float32 [6, 5, 5, 65536], P(None, None, None, ('groups', 'slab')), parts along dimension 3, may hold values from -0.3 to 0.3
- inv_blocks: float32 [5, 5, 65536], P(None, None, ('groups', 'slab')), parts along dimension 2, may hold values from -0.9 to 3, as said below
Outputs:
- modes_basis: float32 [5, 64, 65536], P(None, None, ('groups', 'slab')), parts along dimension 2
- factor: float32 [128, 64], P('groups'), parts along dimension 0
There are 2 independent parts, one for each index of `groups`. A program takes and returns all parts, laid end to end along the dimension named above; each array names one. Nothing has to cross between parts.
Inputs may be any that keep to these rules, and one draw needn't show every extreme that they name: `owner_dev`: in the rows of one slab device at most 64 shell nodes name the same slab, a bound that some of them reach. `neighbours`: A filled slot of cell c names a cell whose number differs from c by 1 to 256. `inv_blocks`: each block has a positive diagonal entry shared by its five diagonal places and off-diagonal entries of at most 0.3 times it in magnitude.
All inputs are finite; a program needn't handle non-finite values.
Results may differ from a plain program's by a relative error of at most 0.0003.
Values sent between devices are 32-bit elements; how exact they have to be, the bound alone decides.
No kernel may reach another device: no remote copies, remote signals or barrier semaphores. Data moves between devices by JAX's collectives and lax.ppermute only.
A program may use at most 192 MiB of HBM per device.

v0:
```python
import math
import jax
import jax.numpy as jnp
from jax import lax
from jax.sharding import PartitionSpec as P

VARS = 5
NBR = 6
SWEEPS = 2


def with_halo(x, sides, width):
    for axis, dim in sides:
        count, length = (lax.axis_size(axis), x.shape[dim])
        up = [(i, (i + 1) % count) for i in range(count - 1)]
        down = [(j, i) for i, j in up]
        last = lax.slice_in_dim(x, length - width, length, axis=dim)
        first = lax.slice_in_dim(x, 0, width, axis=dim)
        before = lax.ppermute(last, axis, up)
        after = lax.ppermute(first, axis, down)
        x = jnp.concatenate([before, x, after], axis=dim)
    return x


def apply_blocks(blocks, field_in):
    rows_out = []
    for out_var in range(field_in.shape[0]):
        summed = blocks[out_var, 0][None, :] * field_in[0]
        for in_var in range(1, field_in.shape[0]):
            summed = summed + blocks[out_var, in_var][None, :] * field_in[in_var]
        rows_out.append(summed)
    return jnp.stack(rows_out)


def couple(weights, shapes):
    node_count = weights.shape[0]
    modes_total = shapes.shape[1] // 3
    weights_split = weights.reshape(node_count, -1, 3)
    shapes_split = shapes.reshape(node_count, 3, modes_total)
    summed = weights_split[:, :, 0, None] * shapes_split[:, None, 0, :]
    for component in range(1, 3):
        summed = summed + weights_split[:, :, component, None] * shapes_split[:, None, component, :]
    return summed.reshape(node_count, -1)


def gram_matrix(left_field, right_field):
    return jnp.einsum("vpc,vqc->pq", left_field, right_field, precision=lax.Precision.HIGHEST)


def combine(coeffs, field_in):
    return jnp.einsum("pq,vpc->vqc", coeffs, field_in, precision=lax.Precision.HIGHEST)


def cholesky_upper(gram):
    order = gram.shape[0]
    places = jnp.arange(order, dtype=jnp.int32)

    def column_step(column_at, lower):
        row_now = lax.dynamic_index_in_dim(lower, column_at, 0, keepdims=False)
        target = lax.dynamic_index_in_dim(gram, column_at, 1, keepdims=False)
        reduced = target - jnp.dot(lower, row_now, precision=lax.Precision.HIGHEST)
        pivot = jnp.sqrt(lax.dynamic_index_in_dim(reduced, column_at, 0, keepdims=False))
        column = jnp.where(
            places > column_at, reduced / pivot, jnp.where(places == column_at, pivot, 0.0)
        )
        return jnp.where(places[None, :] == column_at, column[:, None], lower)

    lower = lax.fori_loop(0, order, column_step, jnp.zeros((order, order), jnp.float32))
    return lower.T


def upper_inverse(upper):
    lower = upper.T
    order = lower.shape[0]
    places = jnp.arange(order, dtype=jnp.int32)
    identity = jnp.eye(order, dtype=jnp.float32)

    def row_step(row_at, inverse):
        lower_row = lax.dynamic_index_in_dim(lower, row_at, 0, keepdims=False)
        pivot = lax.dynamic_index_in_dim(lower_row, row_at, 0, keepdims=False)
        earlier = jnp.where(places < row_at, lower_row, 0.0)
        unit_row = lax.dynamic_index_in_dim(identity, row_at, 0, keepdims=False)
        new_row = (unit_row - jnp.dot(earlier, inverse, precision=lax.Precision.HIGHEST)) / pivot
        return jnp.where(places[:, None] == row_at, new_row[None, :], inverse)

    inverse = lax.fori_loop(0, order, row_step, jnp.zeros((order, order), jnp.float32))
    return inverse.T


def local(
    mode_shapes, wall_coupling, owner_dev, owner_cell, neighbours, coupling_blocks, inv_blocks
):
    devices_slab = lax.axis_size("slab")
    cell_count = inv_blocks.shape[2]
    node_count = mode_shapes.shape[0]
    modes_total = mode_shapes.shape[1] // 3
    capacity = max(2, 2 * node_count // devices_slab)
    destination = owner_dev[:, 0]
    onehot_dest = (
        destination[:, None] == jnp.arange(devices_slab, dtype=jnp.int32)[None, :]
    ).astype(jnp.int32)
    ranking = jnp.sum((jnp.cumsum(onehot_dest, axis=0) - 1) * onehot_dest, axis=1)
    slot_of = destination * capacity + ranking
    slot_total = devices_slab * capacity
    cell_tags = (
        jnp.full((slot_total,), -1.0, jnp.float32).at[slot_of].set(owner_cell.astype(jnp.float32))
    )
    contribution = couple(wall_coupling, mode_shapes)
    outgoing = (
        jnp.zeros((slot_total, contribution.shape[1]), jnp.float32).at[slot_of].set(contribution)
    )
    arrived, arrived_tags = (
        lax.all_to_all(outgoing, "slab", split_axis=0, concat_axis=0, tiled=True),
        lax.all_to_all(cell_tags, "slab", split_axis=0, concat_axis=0, tiled=True),
    )
    matches = (
        arrived_tags.astype(jnp.int32)[:, None] == jnp.arange(cell_count, dtype=jnp.int32)[None, :]
    ).astype(jnp.float32)
    forcing = lax.dot_general(
        arrived, matches, (((0,), (0,)), ((), ())), precision=lax.Precision.HIGHEST
    )
    forcing = forcing.reshape(VARS, modes_total, cell_count)
    rim_width = cell_count // 8
    first_cell = lax.axis_index("slab") * cell_count - rim_width
    local_ids = jnp.where(neighbours >= 0, neighbours - first_cell, cell_count + 2 * rim_width)
    state_field = apply_blocks(inv_blocks, forcing)
    for sweep_step in range(SWEEPS):
        widened = with_halo(state_field, (("slab", 2),), rim_width)
        padded = jnp.concatenate(
            [widened, jnp.zeros(widened.shape[:2] + (1,), jnp.float32)], axis=2
        )
        coupled = jnp.zeros_like(state_field)
        for slot_index in range(NBR):
            gathered = jnp.take(padded, local_ids[slot_index], axis=2)
            coupled = coupled + apply_blocks(coupling_blocks[slot_index], gathered)
        state_field = apply_blocks(inv_blocks, forcing - coupled)
    block_width = modes_total // 4
    factor = jnp.zeros((modes_total, modes_total), jnp.float32)
    basis_parts = []
    for block_index in range(4):
        start_col = block_index * block_width
        panel_cols = state_field[:, start_col : start_col + block_width, :]
        if block_index > 0:
            previous = jnp.concatenate(basis_parts, axis=1)
            projection = lax.psum(gram_matrix(previous, panel_cols), "slab")
            panel_cols = panel_cols - combine(projection, previous)
            factor = factor.at[:start_col, start_col : start_col + block_width].set(projection)
        diag_block = cholesky_upper(lax.psum(gram_matrix(panel_cols, panel_cols), "slab"))
        factor = factor.at[
            start_col : start_col + block_width, start_col : start_col + block_width
        ].set(diag_block)
        basis_parts.append(combine(upper_inverse(diag_block), panel_cols))
    basis_out = jnp.concatenate(basis_parts, axis=1)
    norm_scale = math.sqrt(VARS * cell_count * devices_slab)
    return (basis_out * norm_scale, factor / norm_scale)


def solution(mesh):
    in_specs = (
        P(("groups", "slab"), None),
        P(("groups", "slab"), None),
        P(("groups", "slab"), None),
        P(("groups", "slab")),
        P(None, ("groups", "slab")),
        P(None, None, None, ("groups", "slab")),
        P(None, None, ("groups", "slab")),
    )
    out_specs = (P(None, None, ("groups", "slab")), P("groups", None))
    return jax.shard_map(local, mesh=mesh, in_specs=in_specs, out_specs=out_specs, check_vma=False)
```

profile of v0, /device:TPU:0, one launch (start us, length us, event | category | flops | bytes accessed | tf_op | source)
XLA Modules:
  0.0 1054.8 jit_solution(16598022416229044817)
XLA Ops:
  8.1 7.4 all-to-all-start.1
  52.9 27.0 %all-to-all-done = f32[16,64,320]{2,1,0:T(8,128)S(1)} async-done(((f32[16,64,320]{2,1,0:T(8,128)}), f32[16,64,320]{2,1,0:T(8,128)S(1)}, u32[]{:S(2)}, u32[]{:S(2)}) %all-to-all-start) | async-done | bytes 1310752 | tf_op jit(solution)/shard_map/all_to_all | solution.py:113
  98.3 7.6 copy.130
  105.9 19.7 %gather_fusion.5 = f32[2048,5,64]{2,1,0:T(8,128)} fusion(f32[5,64,2561]{1,0,2:T(8,128)} %copy.130, s32[2048]{0:T(1024)} %get-tuple-element.1568), kind=kCustom, calls=%fused_computation.5.clone | custom fusion | bytes 5251072 | tf_op jit(solution)/shard_map/jit(_take)/gather | solution.py:134
  131.7 19.6 %gather_fusion.4 = f32[2048,5,64]{2,1,0:T(8,128)} fusion(f32[5,64,2561]{1,0,2:T(8,128)} %copy.130, s32[2048]{0:T(1024)S(1)} %copy-done.195), kind=kCustom, calls=%fused_computation.4.clone | custom fusion | bytes 5251072 | tf_op jit(solution)/shard_map/jit(_take)/gather | solution.py:134
  157.4 19.6 %gather_fusion.3 = f32[2048,5,64]{2,1,0:T(8,128)} fusion(f32[5,64,2561]{1,0,2:T(8,128)} %copy.130, s32[2048]{0:T(1024)S(1)} %copy-done.193), kind=kCustom, calls=%fused_computation.3.clone | custom fusion | bytes 5251072 | tf_op jit(solution)/shard_map/jit(_take)/gather | solution.py:134
  183.1 19.6 %gather_fusion.2 = f32[2048,5,64]{2,1,0:T(8,128)} fusion(f32[5,64,2561]{1,0,2:T(8,128)} %copy.130, s32[2048]{0:T(1024)S(1)} %copy-done.198), kind=kCustom, calls=%fused_computation.2.clone | custom fusion | bytes 5251072 | tf_op jit(solution)/shard_map/jit(_take)/gather | solution.py:134
  208.8 19.6 %gather_fusion.1 = f32[2048,5,64]{2,1,0:T(8,128)} fusion(f32[5,64,2561]{1,0,2:T(8,128)} %copy.130, s32[2048]{0:T(1024)S(1)} %copy-done.196), kind=kCustom, calls=%fused_computation.1.clone | custom fusion | bytes 5251072 | tf_op jit(solution)/shard_map/jit(_take)/gather | solution.py:134
  234.5 19.6 %gather_fusion = f32[2048,5,64]{2,1,0:T(8,128)} fusion(f32[5,64,2561]{1,0,2:T(8,128)} %copy.130, s32[2048]{0:T(1024)S(1)} %get-tuple-element.1569), kind=kCustom, calls=%fused_computation.clone | custom fusion | bytes 5251072 | tf_op jit(solution)/shard_map/jit(_take)/gather | solution.py:134
  291.8 7.3 collective-permute-start.2
  304.6 7.6 copy.147
  312.3 19.7 %gather_fusion.11 = f32[2048,5,64]{2,1,0:T(8,128)} fusion(f32[5,64,2561]{1,0,2:T(8,128)} %copy.147, s32[2048]{0:T(1024)} %get-tuple-element.1568), kind=kCustom, calls=%fused_computation.11.clone | custom fusion | bytes 5251072 | tf_op jit(solution)/shard_map/jit(_take)/gather | solution.py:134
  332.0 19.8 %gather_fusion.10 = f32[2048,5,64]{2,1,0:T(8,128)} fusion(f32[5,64,2561]{1,0,2:T(8,128)} %copy.147, s32[2048]{0:T(1024)} %get-tuple-element.1567), kind=kCustom, calls=%fused_computation.10.clone | custom fusion | bytes 5251072 | tf_op jit(solution)/shard_map/jit(_take)/gather | solution.py:134
  351.9 19.7 %gather_fusion.9 = f32[2048,5,64]{2,1,0:T(8,128)} fusion(f32[5,64,2561]{1,0,2:T(8,128)} %copy.147, s32[2048]{0:T(1024)S(1)} %copy-done.194), kind=kCustom, calls=%fused_computation.9.clone | custom fusion | bytes 5251072 | tf_op jit(solution)/shard_map/jit(_take)/gather | solution.py:134
  371.5 19.8 %gather_fusion.8 = f32[2048,5,64]{2,1,0:T(8,128)} fusion(f32[5,64,2561]{1,0,2:T(8,128)} %copy.147, s32[2048]{0:T(1024)} %get-tuple-element.1565), kind=kCustom, calls=%fused_computation.8.clone | custom fusion | bytes 5251072 | tf_op jit(solution)/shard_map/jit(_take)/gather | solution.py:134
  391.4 19.8 %gather_fusion.7 = f32[2048,5,64]{2,1,0:T(8,128)} fusion(f32[5,64,2561]{1,0,2:T(8,128)} %copy.147, s32[2048]{0:T(1024)S(1)} %copy-done.197), kind=kCustom, calls=%fused_computation.7.clone | custom fusion | bytes 5251072 | tf_op jit(solution)/shard_map/jit(_take)/gather | solution.py:134
  411.2 19.7 %gather_fusion.6 = f32[2048,5,64]{2,1,0:T(8,128)} fusion(f32[5,64,2561]{1,0,2:T(8,128)} %copy.147, s32[2048]{0:T(1024)} %copy-done.199), kind=kCustom, calls=%fused_computation.6.clone | custom fusion | bytes 5251072 | tf_op jit(solution)/shard_map/jit(_take)/gather | solution.py:134
  511.8 37.7 %psum.49 = f32[16,16]{1,0:T(8,128)S(1)} all-reduce(f32[16,16]{1,0:T(8,128)S(1)} %convolution_bitcast_fusion.20), channel_id=1, replica_groups=mesh['groups'=2,'slab'=16] {'slab'}, use_global_device_ids=true, to_apply=%region_5.7 | all-reduce | flops 256 | bytes 2048 | tf_op jit(solution)/shard_map/psum | solution.py:148
  549.6 24.4 %while.139 = (s32[]{:T(128)}, f32[16,16]{1,0:T(8,128)S(1)}, f32[16,16]{0,1:T(8,128)S(1)}, s32[]{:T(128)}, s32[]{:T(128)}) while((s32[]{:T(128)}, f32[16,16]{1,0:T(8,128)S(1)}, f32[16,16]{0,1:T(8,128)S(1)}, s32[]{:T(128)}, s32[]{:T(128)}) %tuple.552), condition=%wide.region_7.9_spmd.clone.clone, body=%wide.region_6.8_spmd.clone.clone.sunk | while | flops 3955 | bytes 14736 | solution.py:68
  574.0 34.1 %while.140 = (s32[]{:T(128)}, f32[16,16]{1,0:T(8,128)S(1)}, f32[16,16]{1,0:T(8,128)}, f32[16,16]{1,0:T(8,128)S(1)}, s32[]{:T(128)}, /*index=5*/s32[]{:T(128)}, s32[]{:T(128)}) while((s32[]{:T(128)}, f32[16,16]{1,0:T(8,128)S(1)}, f32[16,16]{1,0:T(8,128)}, f32[16,16]{1,0:T(8,128)S(1)}, s32[]{:T(128)}, ...), condition=%wide.region_9.11_spmd.clone.clone, body=%wide.region_8.10_spmd.clone.clone.sunk | while | flops 3924 | bytes 13155 | solution.py:86
  609.8 30.0 %psum.50 = f32[16,16]{1,0:T(8,128)S(1)} all-reduce(f32[16,16]{1,0:T(8,128)S(1)} %convolution_bitcast_fusion.19), channel_id=1, replica_groups=mesh['groups'=2,'slab'=16] {'slab'}, use_global_device_ids=true, to_apply=%region_10.12 | all-reduce | flops 256 | bytes 2048 | tf_op jit(solution)/shard_map/psum | solution.py:145
  642.6 30.0 %psum.51 = f32[16,16]{1,0:T(8,128)S(1)} all-reduce(f32[16,16]{1,0:T(8,128)S(1)} %convolution_bitcast_fusion.18), channel_id=1, replica_groups=mesh['groups'=2,'slab'=16] {'slab'}, use_global_device_ids=true, to_apply=%region_11.13 | all-reduce | flops 256 | bytes 2048 | tf_op jit(solution)/shard_map/psum | solution.py:148
  672.7 24.4 %while.141 = (s32[]{:T(128)}, f32[16,16]{1,0:T(8,128)S(1)}, f32[16,16]{0,1:T(8,128)S(1)}, s32[]{:T(128)}, s32[]{:T(128)}) while((s32[]{:T(128)}, f32[16,16]{1,0:T(8,128)S(1)}, f32[16,16]{0,1:T(8,128)S(1)}, s32[]{:T(128)}, s32[]{:T(128)}) %tuple.551), condition=%wide.region_13.15_spmd.clone.clone, body=%wide.region_12.14_spmd.clone.clone.sunk | while | flops 3955 | bytes 14736 | solution.py:68
  697.1 34.1 %while.142 = (s32[]{:T(128)}, f32[16,16]{1,0:T(8,128)S(1)}, f32[16,16]{1,0:T(8,128)}, f32[16,16]{1,0:T(8,128)S(1)}, s32[]{:T(128)}, /*index=5*/s32[]{:T(128)}, s32[]{:T(128)}) while((s32[]{:T(128)}, f32[16,16]{1,0:T(8,128)S(1)}, f32[16,16]{1,0:T(8,128)}, f32[16,16]{1,0:T(8,128)S(1)}, s32[]{:T(128)}, ...), condition=%wide.region_15.17_spmd.clone.clone, body=%wide.region_14.16_spmd.clone.clone.sunk | while | flops 3924 | bytes 13155 | solution.py:86
  734.2 57.9 %psum.52 = f32[32,16]{1,0:T(8,128)S(1)} all-reduce(f32[32,16]{1,0:T(8,128)S(1)} %convolution_bitcast_fusion.15), channel_id=1, replica_groups=mesh['groups'=2,'slab'=16] {'slab'}, use_global_device_ids=true, to_apply=%region_16.18 | all-reduce | flops 512 | bytes 4096 | tf_op jit(solution)/shard_map/psum | solution.py:145
  803.9 30.0 %psum.53 = f32[16,16]{1,0:T(8,128)S(1)} all-reduce(f32[16,16]{1,0:T(8,128)S(1)} %convolution_bitcast_fusion.17), channel_id=1, replica_groups=mesh['groups'=2,'slab'=16] {'slab'}, use_global_device_ids=true, to_apply=%region_17.19 | all-reduce | flops 256 | bytes 2048 | tf_op jit(solution)/shard_map/psum | solution.py:148
  834.0 24.4 %while.143 = (s32[]{:T(128)}, f32[16,16]{1,0:T(8,128)S(1)}, f32[16,16]{0,1:T(8,128)S(1)}, s32[]{:T(128)}, s32[]{:T(128)}) while((s32[]{:T(128)}, f32[16,16]{1,0:T(8,128)S(1)}, f32[16,16]{0,1:T(8,128)S(1)}, s32[]{:T(128)}, s32[]{:T(128)}) %tuple.550), condition=%wide.region_19.21_spmd.clone.clone, body=%wide.region_18.20_spmd.clone.clone.sunk | while | flops 3955 | bytes 14736 | solution.py:68
  858.4 34.1 %while.144 = (s32[]{:T(128)}, f32[16,16]{1,0:T(8,128)S(1)}, f32[16,16]{1,0:T(8,128)}, f32[16,16]{1,0:T(8,128)S(1)}, s32[]{:T(128)}, /*index=5*/s32[]{:T(128)}, s32[]{:T(128)}) while((s32[]{:T(128)}, f32[16,16]{1,0:T(8,128)S(1)}, f32[16,16]{1,0:T(8,128)}, f32[16,16]{1,0:T(8,128)S(1)}, s32[]{:T(128)}, ...), condition=%wide.region_21.23_spmd.clone.clone, body=%wide.region_20.22_spmd.clone.clone.sunk | while | flops 3924 | bytes 13155 | solution.py:86
  896.0 57.6 %psum.54 = f32[48,16]{1,0:T(8,128)S(1)} all-reduce(f32[48,16]{1,0:T(8,128)S(1)} %fusion.90), channel_id=1, replica_groups=mesh['groups'=2,'slab'=16] {'slab'}, use_global_device_ids=true, to_apply=%region_22.24 | all-reduce | flops 768 | bytes 6144 | tf_op jit(solution)/shard_map/psum | solution.py:145
  962.0 30.0 %psum.55 = f32[16,16]{1,0:T(8,128)S(1)} all-reduce(f32[16,16]{1,0:T(8,128)S(1)} %convolution_bitcast_fusion.16), channel_id=1, replica_groups=mesh['groups'=2,'slab'=16] {'slab'}, use_global_device_ids=true, to_apply=%region_23.25 | all-reduce | flops 256 | bytes 2048 | tf_op jit(solution)/shard_map/psum | solution.py:148
  992.1 24.4 %while.145 = (s32[]{:T(128)}, f32[16,16]{1,0:T(8,128)S(1)}, f32[16,16]{0,1:T(8,128)S(1)}, s32[]{:T(128)}, s32[]{:T(128)}) while((s32[]{:T(128)}, f32[16,16]{1,0:T(8,128)S(1)}, f32[16,16]{0,1:T(8,128)S(1)}, s32[]{:T(128)}, s32[]{:T(128)}) %tuple.549), condition=%wide.region_25.27_spmd.clone.clone, body=%wide.region_24.26_spmd.clone.clone.sunk | while | flops 3955 | bytes 14736 | solution.py:68
  1016.6 34.1 %while.146 = (s32[]{:T(128)}, f32[16,16]{1,0:T(8,128)S(1)}, f32[16,16]{1,0:T(8,128)}, f32[16,16]{1,0:T(8,128)S(1)}, s32[]{:T(128)}, /*index=5*/s32[]{:T(128)}, s32[]{:T(128)}) while((s32[]{:T(128)}, f32[16,16]{1,0:T(8,128)S(1)}, f32[16,16]{1,0:T(8,128)}, f32[16,16]{1,0:T(8,128)S(1)}, s32[]{:T(128)}, ...), condition=%wide.region_27.29_spmd.clone.clone, body=%wide.region_26.28_spmd.clone.clone.sunk | while | flops 3924 | bytes 13155 | solution.py:86
  (1295 shorter events, 438.7 us)
Async XLA Ops:
  8.1 33.1 %all-to-all-start.1 = ((f32[16,64,1]{1,2,0:T(1,128)}), f32[16,64,1]{1,2,0:T(1,128)S(1)}, u32[]{:S(2)}, u32[]{:S(2)}) async-start(f32[16,64,1]{1,2,0:T(1,128)} %bitcast.16), calls=%async_computation.1 | async-start | bytes 16384 | tf_op jit(solution)/shard_map/all_to_all | solution.py:114
  41.8 38.2 %all-to-all-start = ((f32[16,64,320]{2,1,0:T(8,128)}), f32[16,64,320]{2,1,0:T(8,128)S(1)}, u32[]{:S(2)}, u32[]{:S(2)}) async-start(f32[16,64,320]{2,1,0:T(8,128)} %bitcast.14), calls=%async_computation | async-start | bytes 3145728 | tf_op jit(solution)/shard_map/all_to_all | solution.py:113
  51.6 223.7 %copy-start.129 = (f32[1,1,2048]{2,1,0:T(1,128)}, f32[1,1,2048]{2,1,0:T(1,128)S(1)}, u32[]{:S(2)}) copy-start(f32[1,1,2048]{2,1,0:T(1,128)S(1)} %get-tuple-element.1472) | copy-start | bytes 24580
  51.8 224.3 %copy-start.121 = (f32[1,1,2048]{2,1,0:T(1,128)}, f32[1,1,2048]{2,1,0:T(1,128)S(1)}, u32[]{:S(2)}) copy-start(f32[1,1,2048]{2,1,0:T(1,128)S(1)} %get-tuple-element.1462) | copy-start | bytes 24580
  51.8 224.3 %copy-start.123 = (f32[1,1,2048]{2,1,0:T(1,128)}, f32[1,1,2048]{2,1,0:T(1,128)S(1)}, u32[]{:S(2)}) copy-start(f32[1,1,2048]{2,1,0:T(1,128)S(1)} %get-tuple-element.1463) | copy-start | bytes 24580
  51.8 224.3 %copy-start.125 = (f32[1,1,2048]{2,1,0:T(1,128)}, f32[1,1,2048]{2,1,0:T(1,128)S(1)}, u32[]{:S(2)}) copy-start(f32[1,1,2048]{2,1,0:T(1,128)S(1)} %get-tuple-element.1464) | copy-start | bytes 24580
  51.8 224.3 %copy-start.127 = (f32[1,1,2048]{2,1,0:T(1,128)}, f32[1,1,2048]{2,1,0:T(1,128)S(1)}, u32[]{:S(2)}) copy-start(f32[1,1,2048]{2,1,0:T(1,128)S(1)} %get-tuple-element.1465) | copy-start | bytes 24580
  51.8 224.5 %copy-start.111 = (f32[1,1,2048]{2,1,0:T(1,128)}, f32[1,1,2048]{2,1,0:T(1,128)S(1)}, u32[]{:S(2)}) copy-start(f32[1,1,2048]{2,1,0:T(1,128)S(1)} %get-tuple-element.1457) | copy-start | bytes 24580
  51.8 224.5 %copy-start.113 = (f32[1,1,2048]{2,1,0:T(1,128)}, f32[1,1,2048]{2,1,0:T(1,128)S(1)}, u32[]{:S(2)}) copy-start(f32[1,1,2048]{2,1,0:T(1,128)S(1)} %get-tuple-element.1458) | copy-start | bytes 24580
  51.8 224.5 %copy-start.115 = (f32[1,1,2048]{2,1,0:T(1,128)}, f32[1,1,2048]{2,1,0:T(1,128)S(1)}, u32[]{:S(2)}) copy-start(f32[1,1,2048]{2,1,0:T(1,128)S(1)} %get-tuple-element.1459) | copy-start | bytes 24580
  51.8 224.5 %copy-start.117 = (f32[1,1,2048]{2,1,0:T(1,128)}, f32[1,1,2048]{2,1,0:T(1,128)S(1)}, u32[]{:S(2)}) copy-start(f32[1,1,2048]{2,1,0:T(1,128)S(1)} %get-tuple-element.1460) | copy-start | bytes 24580
  51.8 224.5 %copy-start.119 = (f32[1,1,2048]{2,1,0:T(1,128)}, f32[1,1,2048]{2,1,0:T(1,128)S(1)}, u32[]{:S(2)}) copy-start(f32[1,1,2048]{2,1,0:T(1,128)S(1)} %get-tuple-element.1461) | copy-start | bytes 24580
  51.9 224.7 %copy-start.101 = (f32[1,1,2048]{2,1,0:T(1,128)}, f32[1,1,2048]{2,1,0:T(1,128)S(1)}, u32[]{:S(2)}) copy-start(f32[1,1,2048]{2,1,0:T(1,128)S(1)} %get-tuple-element.1452) | copy-start | bytes 24580
  51.9 224.7 %copy-start.103 = (f32[1,1,2048]{2,1,0:T(1,128)}, f32[1,1,2048]{2,1,0:T(1,128)S(1)}, u32[]{:S(2)}) copy-start(f32[1,1,2048]{2,1,0:T(1,128)S(1)} %get-tuple-element.1453) | copy-start | bytes 24580
  51.9 224.7 %copy-start.105 = (f32[1,1,2048]{2,1,0:T(1,128)}, f32[1,1,2048]{2,1,0:T(1,128)S(1)}, u32[]{:S(2)}) copy-start(f32[1,1,2048]{2,1,0:T(1,128)S(1)} %get-tuple-element.1454) | copy-start | bytes 24580
  51.9 224.7 %copy-start.107 = (f32[1,1,2048]{2,1,0:T(1,128)}, f32[1,1,2048]{2,1,0:T(1,128)S(1)}, u32[]{:S(2)}) copy-start(f32[1,1,2048]{2,1,0:T(1,128)S(1)} %get-tuple-element.1455) | copy-start | bytes 24580
  51.9 224.7 %copy-start.109 = (f32[1,1,2048]{2,1,0:T(1,128)}, f32[1,1,2048]{2,1,0:T(1,128)S(1)}, u32[]{:S(2)}) copy-start(f32[1,1,2048]{2,1,0:T(1,128)S(1)} %get-tuple-element.1456) | copy-start | bytes 24580
  51.9 225.0 %copy-start.91 = (f32[1,1,2048]{2,1,0:T(1,128)}, f32[1,1,2048]{2,1,0:T(1,128)S(1)}, u32[]{:S(2)}) copy-start(f32[1,1,2048]{2,1,0:T(1,128)S(1)} %get-tuple-element.1447) | copy-start | bytes 24580
  51.9 225.0 %copy-start.93 = (f32[1,1,2048]{2,1,0:T(1,128)}, f32[1,1,2048]{2,1,0:T(1,128)S(1)}, u32[]{:S(2)}) copy-start(f32[1,1,2048]{2,1,0:T(1,128)S(1)} %get-tuple-element.1448) | copy-start | bytes 24580
  51.9 225.0 %copy-start.95 = (f32[1,1,2048]{2,1,0:T(1,128)}, f32[1,1,2048]{2,1,0:T(1,128)S(1)}, u32[]{:S(2)}) copy-start(f32[1,1,2048]{2,1,0:T(1,128)S(1)} %get-tuple-element.1449) | copy-start | bytes 24580
  51.9 225.0 %copy-start.97 = (f32[1,1,2048]{2,1,0:T(1,128)}, f32[1,1,2048]{2,1,0:T(1,128)S(1)}, u32[]{:S(2)}) copy-start(f32[1,1,2048]{2,1,0:T(1,128)S(1)} %get-tuple-element.1450) | copy-start | bytes 24580
  51.9 225.0 %copy-start.99 = (f32[1,1,2048]{2,1,0:T(1,128)}, f32[1,1,2048]{2,1,0:T(1,128)S(1)}, u32[]{:S(2)}) copy-start(f32[1,1,2048]{2,1,0:T(1,128)S(1)} %get-tuple-element.1451) | copy-start | bytes 24580
  52.1 225.5 %copy-start.83 = (f32[1,1,2048]{2,1,0:T(1,128)}, f32[1,1,2048]{2,1,0:T(1,128)S(1)}, u32[]{:S(2)}) copy-start(f32[1,1,2048]{2,1,0:T(1,128)S(1)} %get-tuple-element.1437) | copy-start | bytes 24580
  52.1 225.5 %copy-start.85 = (f32[1,1,2048]{2,1,0:T(1,128)}, f32[1,1,2048]{2,1,0:T(1,128)S(1)}, u32[]{:S(2)}) copy-start(f32[1,1,2048]{2,1,0:T(1,128)S(1)} %get-tuple-element.1438) | copy-start | bytes 24580
  52.1 225.5 %copy-start.87 = (f32[1,1,2048]{2,1,0:T(1,128)}, f32[1,1,2048]{2,1,0:T(1,128)S(1)}, u32[]{:S(2)}) copy-start(f32[1,1,2048]{2,1,0:T(1,128)S(1)} %get-tuple-element.1439) | copy-start | bytes 24580
  52.1 225.5 %copy-start.89 = (f32[1,1,2048]{2,1,0:T(1,128)}, f32[1,1,2048]{2,1,0:T(1,128)S(1)}, u32[]{:S(2)}) copy-start(f32[1,1,2048]{2,1,0:T(1,128)S(1)} %get-tuple-element.1440) | copy-start | bytes 24580
  52.1 225.8 %copy-start.79 = (f32[1,1,2048]{2,1,0:T(1,128)}, f32[1,1,2048]{2,1,0:T(1,128)S(1)}, u32[]{:S(2)}) copy-start(f32[1,1,2048]{2,1,0:T(1,128)S(1)} %get-tuple-element.1435) | copy-start | bytes 24580
  52.1 225.8 %copy-start.81 = (f32[1,1,2048]{2,1,0:T(1,128)}, f32[1,1,2048]{2,1,0:T(1,128)S(1)}, u32[]{:S(2)}) copy-start(f32[1,1,2048]{2,1,0:T(1,128)S(1)} %get-tuple-element.1436) | copy-start | bytes 24580
  88.5 5.1 collective-permute-start
  91.2 5.0 collective-permute-start.1
  291.8 10.5 collective-permute-start.2
  299.1 3.5 collective-permute-start.3
  (193 other events, 4023.8 us)
where the time goes:
time: 1070 us; the launch traced here: 1050 us
  local copies, waits for them, and re-layouts  451 us (42%)
  blocking collectives  273 us (26%)
  matrix products  127 us (12%)
  other arithmetic  98.8 us (9%)
  loops' own time  45.6 us (4%)
  waiting for transfers between devices  30 us (3%)
  starting transfers between devices  26.2 us (2%)
    gather x24, local copies, waits for them, and re-layouts, local(): gathered = jnp.take(padded, local_ids[slot_index], axis=2)  310 us
    psum x3, blocking collectives, local(): projection = lax.psum(gram_matrix(previous, panel_cols), 'slab')  146 us
    psum x4, blocking collectives, local(): lax.psum(gram_matrix(panel_cols, panel_cols), 'slab')  128 us
    dot_general x64, matrix products, row_step(): jnp.dot(earlier, inverse, precision=lax.Precision.HIGHEST)  93.2 us
    another operation x4, loops' own time, cholesky_upper(): lax.fori_loop(0, order, column_step, jnp.zeros((order, order), jnp.float32))  45.1 us
    dynamic_slice x64, local copies, waits for them, and re-layouts, column_step(): lax.dynamic_index_in_dim(reduced, column_at, 0, keepdims=False)  38 us
    dynamic_slice x64, local copies, waits for them, and re-layouts, row_step(): pivot = lax.dynamic_index_in_dim(lower_row, row_at, 0, keepdims=False)  37.7 us
    unnamed x68, other arithmetic  29.4 us
  transfers between devices with their start and end apart: 6, of which 3 were waited for; matrix products, arithmetic and copies ran while one was open for 3% of the time, Pallas kernels for 0%

commit v1 on v0

--- a/solution.py
+++ b/solution.py
@@ -1,12 +1,32 @@
+import functools
 import math
 import jax
 import jax.numpy as jnp
 from jax import lax
 from jax.sharding import PartitionSpec as P
+from jax.lax import axis_index, axis_size, ppermute
 
 VARS = 5
 NBR = 6
 SWEEPS = 2
+
+
+def patches_keep_up(z, which_dim, where_dim):
+    step_out, view_out = (axis_size("slab"), axis_index("slab"))
+    main = z.shape[which_dim] // step_out
+    tall = jnp.roll(z, -view_out * main, which_dim)
+    gallery = [lax.slice_in_dim(tall, 0, main, axis=which_dim)]
+    for w in range(1, step_out):
+        prior = lax.slice_in_dim(tall, w * main, (w + 1) * main, axis=which_dim)
+        gallery.append(
+            ppermute(prior, "slab", [(tick, (tick + w) % step_out) for tick in range(step_out)])
+        )
+    left_arr = jnp.concatenate(gallery[::-1], where_dim)
+    low = jnp.roll(left_arr, (view_out + 1) * gallery[0].shape[where_dim], where_dim)
+    return low
+
+
+update_the_loads = functools.partial(patches_keep_up, which_dim=0, where_dim=0)
 
 
 def with_halo(x, sides, width):
@@ -110,7 +130,7 @@
         jnp.zeros((slot_total, contribution.shape[1]), jnp.float32).at[slot_of].set(contribution)
     )
     arrived, arrived_tags = (
-        lax.all_to_all(outgoing, "slab", split_axis=0, concat_axis=0, tiled=True),
+        update_the_loads(outgoing),
         lax.all_to_all(cell_tags, "slab", split_axis=0, concat_axis=0, tiled=True),
     )
     matches = (

time: 1070 us -> 1100 us (1.028)
  starting transfers between devices: 26.2 us -> 59.4 us
    ppermute x0 -> x15, starting transfers between devices: none -> 36.4 us  [patches_keep_up(): ppermute(prior, 'slab', [(tick, (tick + w) % step_out) for tick in range(...]
    ppermute x0 -> x15, waiting for transfers between devices: none -> 29.5 us  [patches_keep_up(): ppermute(prior, 'slab', [(tick, (tick + w) % step_out) for tick in range(...]
    all_to_all x1 -> x0, waiting for transfers between devices: 27 us -> none  [local(): lax.all_to_all(outgoing, 'slab', split_axis=0, concat_axis=0, tiled=True)]
  transfers between devices with their start and end apart: 6 -> 20, of which waited for: 3 -> 12; matrix products, arithmetic and copies ran while one was open for 3% -> 3% of each run, Pallas kernels for 0% -> 0%
where the time goes in v1:
time: 1100 us; the launch traced here: 1090 us
  local copies, waits for them, and re-layouts  456 us (41%)
  blocking collectives  271 us (25%)
  matrix products  125 us (11%)
  other arithmetic  94.5 us (9%)
  starting transfers between devices  59.4 us (5%)
  loops' own time  45.6 us (4%)
  waiting for transfers between devices  35.8 us (3%)
    gather x24, local copies, waits for them, and re-layouts, local(): gathered = jnp.take(padded, local_ids[slot_index], axis=2)  310 us
    psum x3, blocking collectives, local(): projection = lax.psum(gram_matrix(previous, panel_cols), 'slab')  146 us
    psum x4, blocking collectives, local(): lax.psum(gram_matrix(panel_cols, panel_cols), 'slab')  125 us
    dot_general x64, matrix products, row_step(): jnp.dot(earlier, inverse, precision=lax.Precision.HIGHEST)  92.2 us
    another operation x4, loops' own time, cholesky_upper(): lax.fori_loop(0, order, column_step, jnp.zeros((order, order), jnp.float32))  45.1 us
    dynamic_slice x64, local copies, waits for them, and re-layouts, column_step(): lax.dynamic_index_in_dim(reduced, column_at, 0, keepdims=False)  38 us
    dynamic_slice x64, local copies, waits for them, and re-layouts, row_step(): pivot = lax.dynamic_index_in_dim(lower_row, row_at, 0, keepdims=False)  37.7 us
    ppermute x15, starting transfers between devices, patches_keep_up(): ppermute(prior, 'slab', [(tick, (tick + w) % step_out) for tick in range(...  36.4 us
  transfers between devices with their start and end apart: 20, of which 12 were waited for; matrix products, arithmetic and copies ran while one was open for 3% of the time, Pallas kernels for 0%

profile of v1, /device:TPU:0, one launch (start us, length us, event | category | flops | bytes accessed | tf_op | source)
XLA Modules:
  0.0 1089.8 jit_solution(13711698549814982445)
XLA Ops:
  8.0 7.4 all-to-all-start
  136.8 7.7 copy.130
  144.5 19.7 %gather_fusion.5 = f32[2048,5,64]{2,1,0:T(8,128)} fusion(f32[5,64,2561]{1,0,2:T(8,128)} %copy.130, s32[2048]{0:T(1024)S(1)} %get-tuple-element.1584), kind=kCustom, calls=%fused_computation.5.clone | custom fusion | bytes 5251072 | tf_op jit(solution)/shard_map/jit(_take)/gather | solution.py:154
  170.2 19.7 %gather_fusion.4 = f32[2048,5,64]{2,1,0:T(8,128)} fusion(f32[5,64,2561]{1,0,2:T(8,128)} %copy.130, s32[2048]{0:T(1024)S(1)} %copy-done.224), kind=kCustom, calls=%fused_computation.4.clone | custom fusion | bytes 5251072 | tf_op jit(solution)/shard_map/jit(_take)/gather | solution.py:154
  196.1 19.7 %gather_fusion.3 = f32[2048,5,64]{2,1,0:T(8,128)} fusion(f32[5,64,2561]{1,0,2:T(8,128)} %copy.130, s32[2048]{0:T(1024)S(1)} %copy-done.222), kind=kCustom, calls=%fused_computation.3.clone | custom fusion | bytes 5251072 | tf_op jit(solution)/shard_map/jit(_take)/gather | solution.py:154
  221.9 19.7 %gather_fusion.2 = f32[2048,5,64]{2,1,0:T(8,128)} fusion(f32[5,64,2561]{1,0,2:T(8,128)} %copy.130, s32[2048]{0:T(1024)S(1)} %copy-done.227), kind=kCustom, calls=%fused_computation.2.clone | custom fusion | bytes 5251072 | tf_op jit(solution)/shard_map/jit(_take)/gather | solution.py:154
  247.6 19.7 %gather_fusion.1 = f32[2048,5,64]{2,1,0:T(8,128)} fusion(f32[5,64,2561]{1,0,2:T(8,128)} %copy.130, s32[2048]{0:T(1024)S(1)} %copy-done.225), kind=kCustom, calls=%fused_computation.1.clone | custom fusion | bytes 5251072 | tf_op jit(solution)/shard_map/jit(_take)/gather | solution.py:154
  273.4 19.7 %gather_fusion = f32[2048,5,64]{2,1,0:T(8,128)} fusion(f32[5,64,2561]{1,0,2:T(8,128)} %copy.130, s32[2048]{0:T(1024)S(1)} %get-tuple-element.1585), kind=kCustom, calls=%fused_computation.clone | custom fusion | bytes 5251072 | tf_op jit(solution)/shard_map/jit(_take)/gather | solution.py:154
  293.1 6.4 copy.131
  330.4 7.3 collective-permute-start.17
  344.3 7.7 copy.147
  352.0 19.8 %gather_fusion.11 = f32[2048,5,64]{2,1,0:T(8,128)} fusion(f32[5,64,2561]{1,0,2:T(8,128)} %copy.147, s32[2048]{0:T(1024)S(1)} %copy-done.230), kind=kCustom, calls=%fused_computation.11.clone | custom fusion | bytes 5251072 | tf_op jit(solution)/shard_map/jit(_take)/gather | solution.py:154
  371.7 19.9 %gather_fusion.10 = f32[2048,5,64]{2,1,0:T(8,128)} fusion(f32[5,64,2561]{1,0,2:T(8,128)} %copy.147, s32[2048]{0:T(1024)} %get-tuple-element.1583), kind=kCustom, calls=%fused_computation.10.clone | custom fusion | bytes 5251072 | tf_op jit(solution)/shard_map/jit(_take)/gather | solution.py:154
  391.6 19.8 %gather_fusion.9 = f32[2048,5,64]{2,1,0:T(8,128)} fusion(f32[5,64,2561]{1,0,2:T(8,128)} %copy.147, s32[2048]{0:T(1024)S(1)} %copy-done.223), kind=kCustom, calls=%fused_computation.9.clone | custom fusion | bytes 5251072 | tf_op jit(solution)/shard_map/jit(_take)/gather | solution.py:154
  411.4 19.9 %gather_fusion.8 = f32[2048,5,64]{2,1,0:T(8,128)} fusion(f32[5,64,2561]{1,0,2:T(8,128)} %copy.147, s32[2048]{0:T(1024)} %get-tuple-element.1581), kind=kCustom, calls=%fused_computation.8.clone | custom fusion | bytes 5251072 | tf_op jit(solution)/shard_map/jit(_take)/gather | solution.py:154
  431.3 19.8 %gather_fusion.7 = f32[2048,5,64]{2,1,0:T(8,128)} fusion(f32[5,64,2561]{1,0,2:T(8,128)} %copy.147, s32[2048]{0:T(1024)S(1)} %copy-done.226), kind=kCustom, calls=%fused_computation.7.clone | custom fusion | bytes 5251072 | tf_op jit(solution)/shard_map/jit(_take)/gather | solution.py:154
  451.1 19.8 %gather_fusion.6 = f32[2048,5,64]{2,1,0:T(8,128)} fusion(f32[5,64,2561]{1,0,2:T(8,128)} %copy.147, s32[2048]{0:T(1024)} %copy-done.228), kind=kCustom, calls=%fused_computation.6.clone | custom fusion | bytes 5251072 | tf_op jit(solution)/shard_map/jit(_take)/gather | solution.py:154
  550.4 35.4 %psum.49 = f32[16,16]{1,0:T(8,128)S(1)} all-reduce(f32[16,16]{1,0:T(8,128)S(1)} %convolution_bitcast_fusion.20), channel_id=1, replica_groups=mesh['groups'=2,'slab'=16] {'slab'}, use_global_device_ids=true, to_apply=%region_5.8 | all-reduce | flops 256 | bytes 2048 | tf_op jit(solution)/shard_map/psum | solution.py:168
  585.8 24.4 %while.139 = (s32[]{:T(128)}, f32[16,16]{1,0:T(8,128)S(1)}, f32[16,16]{0,1:T(8,128)S(1)}, s32[]{:T(128)}, s32[]{:T(128)}) while((s32[]{:T(128)}, f32[16,16]{1,0:T(8,128)S(1)}, f32[16,16]{0,1:T(8,128)S(1)}, s32[]{:T(128)}, s32[]{:T(128)}) %tuple.567), condition=%wide.region_7.10_spmd.clone.clone, body=%wide.region_6.9_spmd.clone.clone.sunk | while | flops 3955 | bytes 14736 | solution.py:88
  610.3 33.9 %while.140 = (s32[]{:T(128)}, f32[16,16]{1,0:T(8,128)S(1)}, f32[16,16]{1,0:T(8,128)}, f32[16,16]{1,0:T(8,128)S(1)}, s32[]{:T(128)}, /*index=5*/s32[]{:T(128)}, s32[]{:T(128)}) while((s32[]{:T(128)}, f32[16,16]{1,0:T(8,128)S(1)}, f32[16,16]{1,0:T(8,128)}, f32[16,16]{1,0:T(8,128)S(1)}, s32[]{:T(128)}, ...), condition=%wide.region_9.12_spmd.clone.clone, body=%wide.region_8.11_spmd.clone.clone.sunk | while | flops 3924 | bytes 13155 | solution.py:106
  645.8 30.0 %psum.50 = f32[16,16]{1,0:T(8,128)S(1)} all-reduce(f32[16,16]{1,0:T(8,128)S(1)} %convolution_bitcast_fusion.19), channel_id=1, replica_groups=mesh['groups'=2,'slab'=16] {'slab'}, use_global_device_ids=true, to_apply=%region_10.13 | all-reduce | flops 256 | bytes 2048 | tf_op jit(solution)/shard_map/psum | solution.py:165
  678.5 30.0 %psum.51 = f32[16,16]{1,0:T(8,128)S(1)} all-reduce(f32[16,16]{1,0:T(8,128)S(1)} %convolution_bitcast_fusion.18), channel_id=1, replica_groups=mesh['groups'=2,'slab'=16] {'slab'}, use_global_device_ids=true, to_apply=%region_11.14 | all-reduce | flops 256 | bytes 2048 | tf_op jit(solution)/shard_map/psum | solution.py:168
  708.6 24.4 %while.141 = (s32[]{:T(128)}, f32[16,16]{1,0:T(8,128)S(1)}, f32[16,16]{0,1:T(8,128)S(1)}, s32[]{:T(128)}, s32[]{:T(128)}) while((s32[]{:T(128)}, f32[16,16]{1,0:T(8,128)S(1)}, f32[16,16]{0,1:T(8,128)S(1)}, s32[]{:T(128)}, s32[]{:T(128)}) %tuple.566), condition=%wide.region_13.16_spmd.clone.clone, body=%wide.region_12.15_spmd.clone.clone.sunk | while | flops 3955 | bytes 14736 | solution.py:88
  733.0 33.9 %while.142 = (s32[]{:T(128)}, f32[16,16]{1,0:T(8,128)S(1)}, f32[16,16]{1,0:T(8,128)}, f32[16,16]{1,0:T(8,128)S(1)}, s32[]{:T(128)}, /*index=5*/s32[]{:T(128)}, s32[]{:T(128)}) while((s32[]{:T(128)}, f32[16,16]{1,0:T(8,128)S(1)}, f32[16,16]{1,0:T(8,128)}, f32[16,16]{1,0:T(8,128)S(1)}, s32[]{:T(128)}, ...), condition=%wide.region_15.18_spmd.clone.clone, body=%wide.region_14.17_spmd.clone.clone.sunk | while | flops 3924 | bytes 13155 | solution.py:106
  769.9 57.9 %psum.52 = f32[32,16]{1,0:T(8,128)S(1)} all-reduce(f32[32,16]{1,0:T(8,128)S(1)} %convolution_bitcast_fusion.15), channel_id=1, replica_groups=mesh['groups'=2,'slab'=16] {'slab'}, use_global_device_ids=true, to_apply=%region_16.19 | all-reduce | flops 512 | bytes 4096 | tf_op jit(solution)/shard_map/psum | solution.py:165
  839.4 30.0 %psum.53 = f32[16,16]{1,0:T(8,128)S(1)} all-reduce(f32[16,16]{1,0:T(8,128)S(1)} %convolution_bitcast_fusion.17), channel_id=1, replica_groups=mesh['groups'=2,'slab'=16] {'slab'}, use_global_device_ids=true, to_apply=%region_17.20 | all-reduce | flops 256 | bytes 2048 | tf_op jit(solution)/shard_map/psum | solution.py:168
  869.5 24.4 %while.143 = (s32[]{:T(128)}, f32[16,16]{1,0:T(8,128)S(1)}, f32[16,16]{0,1:T(8,128)S(1)}, s32[]{:T(128)}, s32[]{:T(128)}) while((s32[]{:T(128)}, f32[16,16]{1,0:T(8,128)S(1)}, f32[16,16]{0,1:T(8,128)S(1)}, s32[]{:T(128)}, s32[]{:T(128)}) %tuple.565), condition=%wide.region_19.22_spmd.clone.clone, body=%wide.region_18.21_spmd.clone.clone.sunk | while | flops 3955 | bytes 14736 | solution.py:88
  893.9 33.9 %while.144 = (s32[]{:T(128)}, f32[16,16]{1,0:T(8,128)S(1)}, f32[16,16]{1,0:T(8,128)}, f32[16,16]{1,0:T(8,128)S(1)}, s32[]{:T(128)}, /*index=5*/s32[]{:T(128)}, s32[]{:T(128)}) while((s32[]{:T(128)}, f32[16,16]{1,0:T(8,128)S(1)}, f32[16,16]{1,0:T(8,128)}, f32[16,16]{1,0:T(8,128)S(1)}, s32[]{:T(128)}, ...), condition=%wide.region_21.24_spmd.clone.clone, body=%wide.region_20.23_spmd.clone.clone.sunk | while | flops 3924 | bytes 13155 | solution.py:106
  931.3 57.6 %psum.54 = f32[48,16]{1,0:T(8,128)S(1)} all-reduce(f32[48,16]{1,0:T(8,128)S(1)} %fusion.93), channel_id=1, replica_groups=mesh['groups'=2,'slab'=16] {'slab'}, use_global_device_ids=true, to_apply=%region_22.25 | all-reduce | flops 768 | bytes 6144 | tf_op jit(solution)/shard_map/psum | solution.py:165
  997.3 30.0 %psum.55 = f32[16,16]{1,0:T(8,128)S(1)} all-reduce(f32[16,16]{1,0:T(8,128)S(1)} %convolution_bitcast_fusion.16), channel_id=1, replica_groups=mesh['groups'=2,'slab'=16] {'slab'}, use_global_device_ids=true, to_apply=%region_23.26 | all-reduce | flops 256 | bytes 2048 | tf_op jit(solution)/shard_map/psum | solution.py:168
  1027.4 24.4 %while.145 = (s32[]{:T(128)}, f32[16,16]{1,0:T(8,128)S(1)}, f32[16,16]{0,1:T(8,128)S(1)}, s32[]{:T(128)}, s32[]{:T(128)}) while((s32[]{:T(128)}, f32[16,16]{1,0:T(8,128)S(1)}, f32[16,16]{0,1:T(8,128)S(1)}, s32[]{:T(128)}, s32[]{:T(128)}) %tuple.564), condition=%wide.region_25.28_spmd.clone.clone, body=%wide.region_24.27_spmd.clone.clone.sunk | while | flops 3955 | bytes 14736 | solution.py:88
  1051.8 33.9 %while.146 = (s32[]{:T(128)}, f32[16,16]{1,0:T(8,128)S(1)}, f32[16,16]{1,0:T(8,128)}, f32[16,16]{1,0:T(8,128)S(1)}, s32[]{:T(128)}, /*index=5*/s32[]{:T(128)}, s32[]{:T(128)}) while((s32[]{:T(128)}, f32[16,16]{1,0:T(8,128)S(1)}, f32[16,16]{1,0:T(8,128)}, f32[16,16]{1,0:T(8,128)S(1)}, s32[]{:T(128)}, ...), condition=%wide.region_27.30_spmd.clone.clone, body=%wide.region_26.29_spmd.clone.clone.sunk | while | flops 3924 | bytes 13155 | solution.py:106
  (1403 shorter events, 496.1 us)
Async XLA Ops:
  8.0 43.7 %all-to-all-start = ((f32[16,64,1]{1,2,0:T(1,128)}), f32[16,64,1]{1,2,0:T(1,128)}, u32[]{:S(2)}, u32[]{:S(2)}) async-start(f32[16,64,1]{1,2,0:T(1,128)} %bitcast.14), calls=%async_computation | async-start | bytes 16384 | tf_op jit(solution)/shard_map/all_to_all | solution.py:134
  21.9 93.2 %collective-permute-start.14 = (f32[64,320]{1,0:T(8,128)S(1)}, f32[64,320]{1,0:T(8,128)}, u32[]{:S(2)}, u32[]{:S(2)}) collective-permute-start(f32[64,320]{1,0:T(8,128)S(1)} %get-tuple-element.1370), channel_id=1, source_target_pairs={{0,1},{1,2},{2,3},{3,4},{4,5},{5,6},{6,7},{7,8},{8,9},{9,10},{10,1... | collective-permute-start | bytes 245768 | tf_op jit(solution)/shard_map/ppermute | solution.py:22
  22.3 92.0 %collective-permute-start.13 = (f32[64,320]{1,0:T(8,128)S(1)}, f32[64,320]{1,0:T(8,128)}, u32[]{:S(2)}, u32[]{:S(2)}) collective-permute-start(f32[64,320]{1,0:T(8,128)S(1)} %get-tuple-element.1371), channel_id=1, source_target_pairs={{0,2},{1,3},{2,4},{3,5},{4,6},{5,7},{6,8},{7,9},{8,10},{9,11},{10,... | collective-permute-start | bytes 245768 | tf_op jit(solution)/shard_map/ppermute | solution.py:22
  23.9 89.4 %collective-permute-start.12 = (f32[64,320]{1,0:T(8,128)S(1)}, f32[64,320]{1,0:T(8,128)}, u32[]{:S(2)}, u32[]{:S(2)}) collective-permute-start(f32[64,320]{1,0:T(8,128)S(1)} %get-tuple-element.1372), channel_id=1, source_target_pairs={{0,3},{1,4},{2,5},{3,6},{4,7},{5,8},{6,9},{7,10},{8,11},{9,12},{10... | collective-permute-start | bytes 245768 | tf_op jit(solution)/shard_map/ppermute | solution.py:22
  26.2 86.3 %collective-permute-start.11 = (f32[64,320]{1,0:T(8,128)S(1)}, f32[64,320]{1,0:T(8,128)}, u32[]{:S(2)}, u32[]{:S(2)}) collective-permute-start(f32[64,320]{1,0:T(8,128)S(1)} %get-tuple-element.1373), channel_id=1, source_target_pairs={{0,4},{1,5},{2,6},{3,7},{4,8},{5,9},{6,10},{7,11},{8,12},{9,13},{1... | collective-permute-start | bytes 245768 | tf_op jit(solution)/shard_map/ppermute | solution.py:22
  27.6 25.5 %collective-permute-start = (f32[64,320]{1,0:T(8,128)}, f32[64,320]{1,0:T(8,128)}, u32[]{:S(2)}, u32[]{:S(2)}) collective-permute-start(f32[64,320]{1,0:T(8,128)} %get-tuple-element.1384), channel_id=1, source_target_pairs={{0,15},{1,0},{2,1},{3,2},{4,3},{5,4},{6,5},{7,6},{8,7},{9,8},{10,9... | collective-permute-start | bytes 245768 | tf_op jit(solution)/shard_map/ppermute | solution.py:22
  29.6 20.2 %copy-start.233 = (s32[1,2048]{1,0:T(1,128)}, s32[1,2048]{1,0:T(1,128)S(1)}, u32[]{:S(2)}) copy-start(s32[1,2048]{1,0:T(1,128)S(1)} %get-tuple-element.1568) | copy-start | bytes 24580
  53.1 63.0 %copy-start.246 = (s32[1024]{0:T(1024)S(1)}, s32[1024]{0:T(1024)}, u32[]{:S(2)}) copy-start(s32[1024]{0:T(1024)} %convert_element_type.34) | copy-start | bytes 12292
  53.1 4.7 collective-permute-start.1
  57.8 4.0 collective-permute-start.2
  61.8 5.0 collective-permute-start.3
  66.8 6.2 collective-permute-start.4
  73.0 6.3 collective-permute-start.5
  79.3 5.7 collective-permute-start.6
  85.1 7.0 collective-permute-start.7
  92.1 5.8 collective-permute-start.8
  97.9 8.5 collective-permute-start.9
  106.4 6.0 collective-permute-start.10
  122.6 7.5 collective-permute-start.15
  128.2 6.7 collective-permute-start.16
  130.0 143.4 %copy-start.228 = (s32[2048]{0:T(1024)}, s32[2048]{0:T(1024)S(1)}, u32[]{:S(2)}) copy-start(s32[2048]{0:T(1024)S(1)} %get-tuple-element.1585) | copy-start | bytes 24580
  330.4 10.4 collective-permute-start.17
  337.7 4.6 collective-permute-start.18
  549.1 36.7 %copy-start.13 = (f32[16,16]{1,0:T(8,128)S(1)}, f32[16,16]{1,0:T(8,128)}, u32[]{:S(2)}) copy-start(f32[16,16]{1,0:T(8,128)} %custom-call) | copy-start | bytes 3076
  549.1 61.1 %copy-start.17 = (f32[16,16]{1,0:T(8,128)S(1)}, f32[16,16]{1,0:T(8,128)}, u32[]{:S(2)}) copy-start(f32[16,16]{1,0:T(8,128)} %custom-call.1) | copy-start | bytes 3076
  549.4 96.4 %copy-start.6 = (f32[5,64,2048]{2,1,0:T(8,128)}, f32[5,64,2048]{2,1,0:T(8,128)S(1)}, u32[]{:S(2)}) copy-start(f32[5,64,2048]{2,1,0:T(8,128)S(1)} %add_dynamic-update-slice_fusion) | copy-start | bytes 7864324
  644.8 63.8 %copy-start.12 = (f32[16,16]{1,0:T(8,128)S(1)}, f32[16,16]{1,0:T(8,128)}, u32[]{:S(2)}) copy-start(f32[16,16]{1,0:T(8,128)} %custom-call.2) | copy-start | bytes 3076
  644.8 88.2 %copy-start.16 = (f32[16,16]{1,0:T(8,128)S(1)}, f32[16,16]{1,0:T(8,128)}, u32[]{:S(2)}) copy-start(f32[16,16]{1,0:T(8,128)} %custom-call.3) | copy-start | bytes 3076
  767.6 101.9 %copy-start.11 = (f32[16,16]{1,0:T(8,128)S(1)}, f32[16,16]{1,0:T(8,128)}, u32[]{:S(2)}) copy-start(f32[16,16]{1,0:T(8,128)} %custom-call.4) | copy-start | bytes 3076
  769.9 124.1 %copy-start.15 = (f32[16,16]{1,0:T(8,128)S(1)}, f32[16,16]{1,0:T(8,128)}, u32[]{:S(2)}) copy-start(f32[16,16]{1,0:T(8,128)} %custom-call.5) | copy-start | bytes 3076
  931.3 96.1 %copy-start.10 = (f32[16,16]{1,0:T(8,128)S(1)}, f32[16,16]{1,0:T(8,128)}, u32[]{:S(2)}) copy-start(f32[16,16]{1,0:T(8,128)} %custom-call.6) | copy-start | bytes 3076
  988.9 62.9 %copy-start.14 = (f32[16,16]{1,0:T(8,128)S(1)}, f32[16,16]{1,0:T(8,128)}, u32[]{:S(2)}) copy-start(f32[16,16]{1,0:T(8,128)} %custom-call.7) | copy-start | bytes 3076
  (238 other events, 472.3 us)
